TPU v7x, 512 devices: a whole 4x4x16 slice. The times are simulated.
512 devices in a mesh: seq: 64 (over z_lo, y, core), rep: 8 (over x, z_hi).
Axes of the slice: x: 4, y: 4, z: 16 (z_hi: 2, z_lo: 8; z = z_hi * 8 + z_lo), core: 2. Of those that a mesh axis runs over, the one named last changes fastest.
Arguments:
- query_rows: bfloat16 [8, 4096, 8192], P('rep', 'seq'), may hold values from -5 to 5
- unrotated_keys: bfloat16 [8, 4096, 1024], P('rep', 'seq'), may hold values from -5 to 5
- value_projections: bfloat16 [8, 4096, 1024], P('rep', 'seq'), may hold values from -6 to 6
- lengths: int32 [8], P('rep'), may hold values from 1024 to 4096, as said below
- page_table: int32 [8, 512, 1], P('rep', 'seq'), may hold values from 0 to 7; in each aligned block of 8 rows (0 to 7, 8 to 15, ..., all dimensions but the last counted through in order) at most 2 rows name the same one
Outputs:
- attended: bfloat16 [8, 4096, 8192], P('rep', 'seq')
- restored_pages: bfloat16 [8, 64, 8, 2, 8, 2048], P('rep', 'seq')
Inputs may be any that keep to these rules, and one draw needn't show every extreme that they name: `lengths`: the longest request of every draw has exactly 4096 tokens. `page_table`: among the 8 pages of one token shard of a request, no owner is named more than 2 times, and in every draw some owner is named exactly 2 times in some shard.
All inputs are finite; a program needn't handle non-finite values.
Results may differ from a plain program's by a relative error of at most 0.011.
Values may be sent and summed in bfloat16 or wider, within the bound.
A program may use at most 64 MiB of HBM per device.

v0:
```python
import math

import jax
import jax.numpy as jnp
from jax import lax
from jax.sharding import PartitionSpec as P

QUERY_HEAD_COUNT = 64
KEY_VALUE_HEADS = 8
HEAD_SIZE = 128


def rotary_embed(values_in, token_positions):
    halfwidth = HEAD_SIZE // 2
    frequency = jnp.exp(
        -jnp.arange(halfwidth, dtype=jnp.float32) * (2.0 * math.log(500000.0) / HEAD_SIZE)
    )
    angles = token_positions.astype(jnp.float32)[:, None] * frequency[None, :]
    cosine = jnp.cos(angles)[:, None, :]
    sine_part = jnp.sin(angles)[:, None, :]
    first_half = values_in[..., :halfwidth]
    second_half = values_in[..., halfwidth:]
    return jnp.concatenate(
        [
            first_half * cosine - second_half * sine_part,
            second_half * cosine + first_half * sine_part,
        ],
        axis=-1,
    )


def slot_table(owner_ids, owners, capacity):
    targets = jnp.arange(owners, dtype=jnp.int32)
    matches = (owner_ids[None, :, :] == targets[:, None, None]).astype(jnp.int32)
    earlier = jnp.cumsum(matches, axis=-1) - matches
    slot_ids = jnp.arange(capacity, dtype=jnp.int32)
    chosen = (matches[:, :, None, :] == 1) & (
        earlier[:, :, None, :] == slot_ids[None, None, :, None]
    )
    return chosen.astype(jnp.float32)


def send_pages(cache_entries, table_shard):
    page_count = table_shard.shape[1]
    owners = lax.axis_size("rep")
    capacity = max(2, 2 * page_count // owners)
    chosen = slot_table(table_shard[:, :, 0], owners, capacity)[:, 0].astype(jnp.bfloat16)
    page_rows = cache_entries.reshape(page_count, -1)
    outgoing = jnp.einsum(
        "ocj,jx->ocx", chosen, page_rows, preferred_element_type=jnp.float32
    ).astype(jnp.bfloat16)
    incoming = lax.all_to_all(outgoing, "rep", split_axis=0, concat_axis=0, tiled=True)
    return incoming.reshape(
        1, 1, owners, capacity, cache_entries.shape[0] // page_count, cache_entries.shape[1]
    )


def attend_heads(query_heads, key_heads, value_head_rows, length, block_rows):
    total_rows = query_heads.shape[0]
    head_count = query_heads.shape[1]
    head_width = query_heads.shape[2]
    score_scale = 1.0 / math.sqrt(head_width)
    offsets = jnp.arange(block_rows, dtype=jnp.int32)

    def query_block(block_index):
        start_row = block_index * block_rows
        query_part = lax.dynamic_slice_in_dim(query_heads, start_row, block_rows, 0)
        query_positions = start_row + offsets

        def key_step(key_index, state_carry):
            running_max, running_sum, running_out = state_carry
            key_start = key_index * block_rows
            key_part = lax.dynamic_slice_in_dim(key_heads, key_start, block_rows, 0)
            value_part = lax.dynamic_slice_in_dim(value_head_rows, key_start, block_rows, 0)
            key_positions = key_start + offsets
            allowed = (key_positions[None, :] <= query_positions[:, None]) & (
                key_positions[None, :] < length
            )
            scores = jnp.einsum(
                "qhd,kd->hqk", query_part, key_part[:, 0], preferred_element_type=jnp.float32
            )
            scores = jnp.where(allowed[None], scores * score_scale, -1e30)
            new_max = jnp.maximum(running_max, jnp.max(scores, axis=-1))
            rescale = jnp.exp(running_max - new_max)
            weights = jnp.where(allowed[None], jnp.exp(scores - new_max[..., None]), 0.0)
            new_sum = running_sum * rescale + jnp.sum(weights, axis=-1)
            contrib = jnp.einsum(
                "hqk,kd->hqd",
                weights.astype(jnp.bfloat16),
                value_part[:, 0],
                preferred_element_type=jnp.float32,
            )
            return (new_max, new_sum, running_out * rescale[..., None] + contrib)

        initial = (
            jnp.full((head_count, block_rows), -1e30, jnp.float32),
            jnp.zeros((head_count, block_rows), jnp.float32),
            jnp.zeros((head_count, block_rows, head_width), jnp.float32),
        )
        final_max, final_sum, final_out = lax.fori_loop(0, block_index + 1, key_step, initial)
        result = final_out / final_sum[..., None]
        result = jnp.where((query_positions < length)[None, :, None], result, 0.0)
        return jnp.transpose(result, (1, 0, 2)).astype(jnp.bfloat16)

    outputs = lax.map(query_block, jnp.arange(total_rows // block_rows, dtype=jnp.int32))
    return outputs.reshape(total_rows, head_count, head_width)


def body(query_rows, unrotated_keys, value_projections, lengths, page_table):
    shard_count = lax.axis_size("seq")
    shard_rows = query_rows.shape[1]
    total_rows = shard_rows * shard_count
    group_width = QUERY_HEAD_COUNT // KEY_VALUE_HEADS
    length = lengths[0]
    my_index = lax.axis_index("seq")
    token_positions = my_index * shard_rows + jnp.arange(shard_rows, dtype=jnp.int32)
    rotated_q = rotary_embed(
        query_rows[0].astype(jnp.float32).reshape(shard_rows, QUERY_HEAD_COUNT, HEAD_SIZE),
        token_positions,
    ).astype(jnp.bfloat16)
    rotated_keys = rotary_embed(
        unrotated_keys[0].astype(jnp.float32).reshape(shard_rows, KEY_VALUE_HEADS, HEAD_SIZE),
        token_positions,
    ).astype(jnp.bfloat16)
    value_shard = value_projections[0].reshape(shard_rows, KEY_VALUE_HEADS, HEAD_SIZE)
    in_length = token_positions < length
    cache_entries = jnp.concatenate(
        [rotated_keys.reshape(shard_rows, KEY_VALUE_HEADS * HEAD_SIZE), value_projections[0]],
        axis=-1,
    )
    cache_entries = jnp.where(in_length[:, None], cache_entries, jnp.zeros_like(cache_entries))
    restored_pages = send_pages(cache_entries, page_table)
    paired = jnp.concatenate([rotated_keys, value_shard], axis=-1)
    widened = jnp.repeat(paired, group_width, axis=1)
    query_heads, pair_heads = (
        lax.all_to_all(rotated_q, "seq", split_axis=1, concat_axis=0, tiled=True),
        lax.all_to_all(widened, "seq", split_axis=1, concat_axis=0, tiled=True),
    )
    key_heads = pair_heads[:, :, :HEAD_SIZE]
    value_head_rows = pair_heads[:, :, HEAD_SIZE:]
    attended_heads = attend_heads(
        query_heads, key_heads, value_head_rows, length, min(512, total_rows)
    )
    returned = lax.all_to_all(attended_heads, "seq", split_axis=0, concat_axis=1, tiled=True)
    return (returned.reshape(1, shard_rows, QUERY_HEAD_COUNT * HEAD_SIZE), restored_pages)


def solution(mesh):
    return jax.shard_map(
        body,
        mesh=mesh,
        in_specs=(
            P("rep", "seq", None),
            P("rep", "seq", None),
            P("rep", "seq", None),
            P("rep"),
            P("rep", "seq", None),
        ),
        out_specs=(P("rep", "seq", None), P("rep", "seq", None, None, None, None)),
        check_vma=False,
    )
```

profile of v0, /device:TPU:481, one launch (start us, length us, event | category | flops | bytes accessed | tf_op | source)
XLA Modules:
  0.0 419.5 jit_solution(16823060860222449509)
XLA Ops:
  3.2 1.6 broadcast_in_dim.38
  4.8 13.8 %all-to-all-start.1 = ((bf16[64,64,256]{2,0,1:T(8,128)(2,1)}), bf16[64,64,256]{2,0,1:T(8,128)(2,1)S(1)}, u32[]{:S(2)}, u32[]{:S(2)}) async-start(bf16[64,64,256]{2,0,1:T(8,128)(2,1)} %bitcast.107), calls=%async_computation.1 | async-start | bytes 4194304 | tf_op jit(solution)/shard_map/all_to_all | solution.py:137
  20.6 1.7 copy.21
  22.3 87.1 %all-to-all-done.1 = bf16[64,64,256]{2,0,1:T(8,128)(2,1)S(1)} async-done(((bf16[64,64,256]{2,0,1:T(8,128)(2,1)}), bf16[64,64,256]{2,0,1:T(8,128)(2,1)S(1)}, u32[]{:S(2)}, u32[]{:S(2)}) %all-to-all-start.1) | async-done | bytes 2097184 | tf_op jit(solution)/shard_map/all_to_all | solution.py:137
  109.4 13.4 %all-to-all-start = ((bf16[64,64,128]{2,0,1:T(8,128)(2,1)}), bf16[64,64,128]{2,0,1:T(8,128)(2,1)S(1)}, u32[]{:S(2)}, u32[]{:S(2)}) async-start(bf16[64,64,128]{2,0,1:T(8,128)(2,1)} %copy.21), calls=%async_computation | async-start | bytes 2097152 | tf_op jit(solution)/shard_map/all_to_all | solution.py:136
  125.9 1.3 copy.25
  127.2 1.5 fusion.33
  128.7 40.0 %all-to-all-done = bf16[64,64,128]{2,0,1:T(8,128)(2,1)S(1)} async-done(((bf16[64,64,128]{2,0,1:T(8,128)(2,1)}), bf16[64,64,128]{2,0,1:T(8,128)(2,1)S(1)}, u32[]{:S(2)}, u32[]{:S(2)}) %all-to-all-start) | async-done | bytes 1048608 | tf_op jit(solution)/shard_map/all_to_all | solution.py:136
  168.7 13.9 %all-to-all-start.3 = ((bf16[8,2,16384]{2,1,0:T(2,128)(2,1)}), bf16[8,2,16384]{2,1,0:T(2,128)(2,1)S(1)}, u32[]{:S(2)}, u32[]{:S(2)}) async-start(bf16[8,2,16384]{2,1,0:T(2,128)(2,1)} %copy.25), calls=%async_computation.3 | async-start | bytes 1048576 | tf_op jit(solution)/shard_map/all_to_all | solution.py:52
  182.6 169.6 %while.29 = (s32[]{:T(128)}, bf16[8,512,1,128]{3,1,2,0:T(8,128)(2,1)}, s32[8]{0:T(128)S(1)}, s32[]{:T(128)}, bf16[4096,1,128]{2,0,1:T(8,128)(2,1)S(1)}, /*index=...) while((s32[]{:T(128)}, ...), condition=%wide.region_5.6_spmd.clone.clone, body=%wide.region_0.5_spmd.clone.clone.sunk | while | flops 138481152 | bytes 5043814 | solution.py:105
  184.3 4.0 while.30
  186.7 1.6 fusion.43
  191.6 8.0 %while.30 = (s32[]{:T(128)}, f32[1,512]{1,0:T(1,128)S(1)}, f32[1,512]{1,0:T(1,128)S(1)}, f32[1,512,128]{2,1,0:T(8,128)S(1)}, s32[]{:T(128)}, /*index=5*/s32[512]...) while((s32[]{:T(128)}, f32[1,512]{1,0:T(1,128)S(1)}, ...), condition=%wide.region_4.4_spmd, body=%wide.region_1.3_spmd.sunk | while | flops 138283008 | bytes 4114643 | solution.py:100
  194.0 1.6 fusion.43
  198.0 1.6 fusion.43
  202.9 11.9 %while.30 = (s32[]{:T(128)}, f32[1,512]{1,0:T(1,128)S(1)}, f32[1,512]{1,0:T(1,128)S(1)}, f32[1,512,128]{2,1,0:T(8,128)S(1)}, s32[]{:T(128)}, /*index=5*/s32[512]...) while((s32[]{:T(128)}, f32[1,512]{1,0:T(1,128)S(1)}, ...), condition=%wide.region_4.4_spmd, body=%wide.region_1.3_spmd.sunk | while | flops 138283008 | bytes 4114643 | solution.py:100
  205.3 1.6 fusion.43
  209.2 1.6 fusion.43
  213.2 1.6 fusion.43
  218.1 15.9 %while.30 = (s32[]{:T(128)}, f32[1,512]{1,0:T(1,128)S(1)}, f32[1,512]{1,0:T(1,128)S(1)}, f32[1,512,128]{2,1,0:T(8,128)S(1)}, s32[]{:T(128)}, /*index=5*/s32[512]...) while((s32[]{:T(128)}, f32[1,512]{1,0:T(1,128)S(1)}, ...), condition=%wide.region_4.4_spmd, body=%wide.region_1.3_spmd.sunk | while | flops 138283008 | bytes 4114643 | solution.py:100
  218.8 1.3 fusion.41
  220.5 1.6 fusion.43
  224.5 1.6 fusion.43
  228.5 1.6 fusion.43
  232.4 1.6 fusion.43
  237.3 19.9 %while.30 = (s32[]{:T(128)}, f32[1,512]{1,0:T(1,128)S(1)}, f32[1,512]{1,0:T(1,128)S(1)}, f32[1,512,128]{2,1,0:T(8,128)S(1)}, s32[]{:T(128)}, /*index=5*/s32[512]...) while((s32[]{:T(128)}, f32[1,512]{1,0:T(1,128)S(1)}, ...), condition=%wide.region_4.4_spmd, body=%wide.region_1.3_spmd.sunk | while | flops 138283008 | bytes 4114643 | solution.py:100
  238.0 1.3 fusion.41
  239.7 1.6 fusion.43
  243.7 1.6 fusion.43
  247.7 1.6 fusion.43
  251.6 1.6 fusion.43
  253.9 1.3 fusion.41
  255.6 1.6 fusion.43
  260.5 23.9 %while.30 = (s32[]{:T(128)}, f32[1,512]{1,0:T(1,128)S(1)}, f32[1,512]{1,0:T(1,128)S(1)}, f32[1,512,128]{2,1,0:T(8,128)S(1)}, s32[]{:T(128)}, /*index=5*/s32[512]...) while((s32[]{:T(128)}, f32[1,512]{1,0:T(1,128)S(1)}, ...), condition=%wide.region_4.4_spmd, body=%wide.region_1.3_spmd.sunk | while | flops 138283008 | bytes 4114643 | solution.py:100
  262.9 1.6 fusion.43
  265.2 1.3 fusion.41
  266.9 1.6 fusion.43
  269.1 1.3 fusion.41
  270.9 1.6 fusion.43
  274.8 1.6 fusion.43
  278.8 1.6 fusion.43
  282.8 1.6 fusion.43
  287.7 27.9 %while.30 = (s32[]{:T(128)}, f32[1,512]{1,0:T(1,128)S(1)}, f32[1,512]{1,0:T(1,128)S(1)}, f32[1,512,128]{2,1,0:T(8,128)S(1)}, s32[]{:T(128)}, /*index=5*/s32[512]...) while((s32[]{:T(128)}, f32[1,512]{1,0:T(1,128)S(1)}, ...), condition=%wide.region_4.4_spmd, body=%wide.region_1.3_spmd.sunk | while | flops 138283008 | bytes 4114643 | solution.py:100
  290.1 1.6 fusion.43
  294.1 1.6 fusion.43
  298.0 1.6 fusion.43
  302.0 1.6 fusion.43
  304.3 1.3 fusion.41
  306.0 1.6 fusion.43
  310.0 1.6 fusion.43
  314.0 1.6 fusion.43
  318.8 31.8 %while.30 = (s32[]{:T(128)}, f32[1,512]{1,0:T(1,128)S(1)}, f32[1,512]{1,0:T(1,128)S(1)}, f32[1,512,128]{2,1,0:T(8,128)S(1)}, s32[]{:T(128)}, /*index=5*/s32[512]...) while((s32[]{:T(128)}, f32[1,512]{1,0:T(1,128)S(1)}, ...), condition=%wide.region_4.4_spmd, body=%wide.region_1.3_spmd.sunk | while | flops 138283008 | bytes 4114643 | solution.py:100
  321.2 1.6 fusion.43
  325.2 1.6 fusion.43
  329.2 1.6 fusion.43
  333.2 1.6 fusion.43
  335.4 1.3 fusion.41
  337.1 1.6 fusion.43
  341.1 1.6 fusion.43
  345.1 1.6 fusion.43
  349.1 1.6 fusion.43
  352.8 2.6 reduce.2
  356.5 14.0 %all-to-all-start.2 = ((bf16[64,2,4096]{2,1,0:T(2,128)(2,1)}), bf16[64,2,4096]{2,1,0:T(2,128)(2,1)S(1)}, u32[]{:S(2)}, u32[]{:S(2)}) async-start(bf16[64,2,4096]{2,1,0:T(2,128)(2,1)} %reshape.301), calls=%async_computation.2 | async-start | bytes 2097152 | tf_op jit(solution)/shard_map/all_to_all | solution.py:144
  371.7 44.7 %all-to-all-done.2 = bf16[64,2,4096]{2,1,0:T(2,128)(2,1)S(1)} async-done(((bf16[64,2,4096]{2,1,0:T(2,128)(2,1)}), bf16[64,2,4096]{2,1,0:T(2,128)(2,1)S(1)}, u32[]{:S(2)}, u32[]{:S(2)}) %all-to-all-start.2) | async-done | bytes 1048608 | tf_op jit(solution)/shard_map/all_to_all | solution.py:144
  (320 shorter events, 105.1 us)
Async XLA Ops:
  4.8 13.8 %copy-start = (bf16[1,64,8192]{2,1,0:T(8,128)(2,1)S(1)}, bf16[1,64,8192]{2,1,0:T(8,128)(2,1)}, u32[]{:S(2)}) copy-start(bf16[1,64,8192]{2,1,0:T(8,128)(2,1)} %param.9) | copy-start | bytes 3145732
  4.8 104.6 %all-to-all-start.1 = ((bf16[64,64,256]{2,0,1:T(8,128)(2,1)}), bf16[64,64,256]{2,0,1:T(8,128)(2,1)S(1)}, u32[]{:S(2)}, u32[]{:S(2)}) async-start(bf16[64,64,256]{2,0,1:T(8,128)(2,1)} %bitcast.107), calls=%async_computation.1 | async-start | bytes 4194304 | tf_op jit(solution)/shard_map/all_to_all | solution.py:137
  20.6 102.9 %copy-start.1 = (bf16[1,64,1024]{2,1,0:T(8,128)(2,1)S(1)}, bf16[1,64,1024]{2,1,0:T(8,128)(2,1)}, u32[]{:S(2)}) copy-start(bf16[1,64,1024]{2,1,0:T(8,128)(2,1)} %param.11) | copy-start | bytes 393220
  22.3 102.1 %copy-start.2 = (s32[1,8,1]{1,2,0:T(1,128)S(1)}, s32[1,8,1]{1,2,0:T(1,128)}, u32[]{:S(2)}) copy-start(s32[1,8,1]{1,2,0:T(1,128)} %param.13) | copy-start | bytes 100
  109.4 59.3 %all-to-all-start = ((bf16[64,64,128]{2,0,1:T(8,128)(2,1)}), bf16[64,64,128]{2,0,1:T(8,128)(2,1)S(1)}, u32[]{:S(2)}, u32[]{:S(2)}) async-start(bf16[64,64,128]{2,0,1:T(8,128)(2,1)} %copy.21), calls=%async_computation | async-start | bytes 2097152 | tf_op jit(solution)/shard_map/all_to_all | solution.py:136
  168.7 187.8 %all-to-all-start.3 = ((bf16[8,2,16384]{2,1,0:T(2,128)(2,1)}), bf16[8,2,16384]{2,1,0:T(2,128)(2,1)S(1)}, u32[]{:S(2)}, u32[]{:S(2)}) async-start(bf16[8,2,16384]{2,1,0:T(2,128)(2,1)} %copy.25), calls=%async_computation.3 | async-start | bytes 1048576 | tf_op jit(solution)/shard_map/all_to_all | solution.py:52
  356.5 59.8 %all-to-all-start.2 = ((bf16[64,2,4096]{2,1,0:T(2,128)(2,1)}), bf16[64,2,4096]{2,1,0:T(2,128)(2,1)S(1)}, u32[]{:S(2)}, u32[]{:S(2)}) async-start(bf16[64,2,4096]{2,1,0:T(2,128)(2,1)} %reshape.301), calls=%async_computation.2 | async-start | bytes 2097152 | tf_op jit(solution)/shard_map/all_to_all | solution.py:144
where the time goes:
time: 427 us; the launch traced here: 420 us
  waiting for transfers between devices  172 us (40%)
  matrix products  105 us (25%)
  other arithmetic  55.3 us (13%)
  starting transfers between devices  55.1 us (13%)
  local copies, waits for them, and re-layouts  19.3 us (5%)
  loops' own time  11.4 us (3%)
    all_to_all x1, waiting for transfers between devices, body(): lax.all_to_all(widened, 'seq', split_axis=1, concat_axis=0, tiled=True)  87.1 us
    dot_general x36, matrix products, key_step(): jnp.einsum('hqk,kd->hqd', weights.astype(jnp.bfloat16), value_part[:, 0],...  56.8 us
    dot_general x36, matrix products, key_step(): jnp.einsum('qhd,kd->hqk', query_part, key_part[:, 0], preferred_element_t...  47.1 us
    all_to_all x1, waiting for transfers between devices, body(): lax.all_to_all(attended_heads, 'seq', split_axis=0, concat_axis=1, tiled=...  44.7 us
    all_to_all x1, waiting for transfers between devices, body(): lax.all_to_all(rotated_q, 'seq', split_axis=1, concat_axis=0, tiled=True)  40 us
    lt x36, other arithmetic, key_step(): key_positions[None, :] < length  23.5 us
    all_to_all x1, starting transfers between devices, body(): lax.all_to_all(attended_heads, 'seq', split_axis=0, concat_axis=1, tiled=...  14 us
    all_to_all x1, starting transfers between devices, send_pages(): lax.all_to_all(outgoing, 'rep', split_axis=0, concat_axis=0, tiled=True)  13.9 us
  transfers between devices with their start and end apart: 4, of which 3 were waited for; matrix products, arithmetic and copies ran while one was open for 41% of the time, Pallas kernels for 0%

commit v1 on v0

v1 whole, which is shorter than its diff:
```python
import functools
import math

import jax
import jax.numpy as jnp
from jax import lax
from jax.experimental import pallas as pl
from jax.experimental.pallas import tpu as pltpu
from jax.sharding import PartitionSpec as P

HEAD = 128
PAGE = 8
SLOTS = 2
SLOT_ROWS = SLOTS * PAGE
Z_HALVES = 2
SCALE = math.log2(math.e) / math.sqrt(HEAD)
MESH = pl.DeviceIdType.MESH
NT = (((1,), (1,)), ((), ()))


def rotary_tables(token_positions):
    halfwidth = HEAD // 2
    frequency = jnp.exp(
        -jnp.arange(halfwidth, dtype=jnp.float32) * (2.0 * math.log(500000.0) / HEAD)
    )
    angles = token_positions.astype(jnp.float32)[:, None] * frequency[None, :]
    cosine, sine = jnp.cos(angles), jnp.sin(angles)
    return (
        jnp.concatenate([cosine, cosine], axis=-1),
        jnp.concatenate([-sine, sine], axis=-1),
    )


def kernel(
    groups, zs, xs,
    q_ref, k_ref, v_ref, cos_ref, sin_ref, len_ref, table_ref,
    o_ref, pages_ref,
    kv_out, kv_all, q_out, q_mine, o_mine, acc, top, pages_out, pages_mid,
    kv_ss, kv_rs, q_ss, q_rs, o_ss, o_rs, z_ss, z_rs, x_ss, x_rs,
    mid_ss, mid_rs, far_ss, far_rs, local_sem,
):
    tokens = q_ref.shape[0]
    rows = groups * tokens
    heads = q_ref.shape[1] // (groups * HEAD)
    wide = heads * HEAD
    half = rows // 2
    span = 2 * zs
    hop = zs // 2
    seq, rep = lax.axis_index("seq"), lax.axis_index("rep")
    z, g = seq // groups, lax.rem(seq, groups)
    x, z_hi = rep // 2, lax.rem(rep, 2)
    z_abs = z_hi * zs + z

    def peer(d):
        return (z * groups + d, rep)

    def along_z(shift, x_at):
        to = lax.rem(z_abs + shift + span, span)
        return (lax.rem(to, zs) * groups + g, x_at * 2 + to // zs)

    def remote(src, dst, ss, rs, device):
        return pltpu.make_async_remote_copy(
            src_ref=src, dst_ref=dst, send_sem=ss, recv_sem=rs,
            device_id=device, device_id_type=MESH,
        )

    barrier = pltpu.get_barrier_semaphore()

    def greet(device):
        pl.semaphore_signal(barrier, inc=1, device_id=device, device_id_type=MESH)

    for i in range(1, groups):
        greet(peer(lax.rem(g + i, groups)))
    for i in range(1, xs):
        greet((seq, lax.rem(x + i, xs) * 2 + z_hi))
    for i in range(xs):
        greet(along_z(hop, i))

    @pl.when(z > 0)
    def _():
        greet((seq - groups, rep))

    cosine, sine = cos_ref[...], sin_ref[...]

    def rotate(head):
        head = head.astype(jnp.float32)
        return (head * cosine + pltpu.roll(head, HEAD // 2, axis=1) * sine).astype(jnp.bfloat16)

    for d in range(groups):
        kv_out[d, :, 0:HEAD] = rotate(k_ref[:, d * HEAD:(d + 1) * HEAD])
        kv_out[d, :, HEAD:2 * HEAD] = v_ref[:, d * HEAD:(d + 1) * HEAD]
    my_rows = pl.ds(pl.multiple_of(g * tokens, tokens), tokens)
    kv_all[z, my_rows, :] = kv_out[g]

    partners = (groups - 1) + (xs - 1) + xs
    pl.semaphore_wait(barrier, partners + jnp.where(z < zs - 1, 1, 0))

    def kv_copy(d, row_of):
        return remote(
            kv_out.at[d],
            kv_all.at[z, pl.ds(pl.multiple_of(row_of * tokens, tokens), tokens)],
            kv_ss.at[d], kv_rs.at[row_of], peer(d),
        )

    for i in range(1, groups):
        kv_copy(lax.rem(g + i, groups), g).start()

    length = len_ref[0]
    owners = [table_ref[j] for j in range(tokens // PAGE)]
    lane = lax.broadcasted_iota(jnp.int32, (1, tokens), 1)
    target = jnp.full((1, tokens), -1, jnp.int32)
    for j, owner in enumerate(owners):
        earlier = jnp.int32(0)
        for i in range(j):
            earlier = earlier + jnp.where(owners[i] == owner, 1, 0)
        owner_x = owner >> 1
        other = jnp.where((owner & 1) == z_hi, 0, xs)
        base = (other + owner_x) * SLOT_ROWS + earlier * PAGE - j * PAGE
        target = jnp.where(
            (lane >= j * PAGE) & (lane < (j + 1) * PAGE) & (earlier < SLOTS), lane + base, target
        )
    target = jnp.where(seq * tokens + lane < length, target, -1)
    slot = lax.broadcasted_iota(jnp.int32, (2 * xs * SLOT_ROWS, tokens), 0)
    chosen = jnp.where(slot == target, 1.0, 0.0).astype(jnp.bfloat16)
    for d in range(groups):
        for part in range(2):
            column = (part * groups + d) * HEAD
            pages_out[:, column:column + HEAD] = jnp.dot(
                chosen, kv_out[d, :, part * HEAD:(part + 1) * HEAD],
                preferred_element_type=jnp.float32,
            ).astype(jnp.bfloat16)

    def slot_rows(i):
        return pl.ds(pl.multiple_of(i * SLOT_ROWS, SLOT_ROWS), SLOT_ROWS)

    def mid_copy(i):
        return remote(
            pages_out.at[slot_rows(xs + i)], pages_mid.at[slot_rows(i)],
            mid_ss.at[i], mid_rs.at[i], along_z(-hop, x),
        )

    def far_copy(i, x_from):
        origin = lax.rem(z_abs + hop, span)
        return remote(
            pages_mid.at[slot_rows(i)], pages_ref.at[slot_rows(x_from * 2 + origin // zs)],
            far_ss.at[i], far_rs.at[x_from], along_z(-hop, i),
        )

    def x_copy(i, x_from):
        return remote(
            pages_out.at[slot_rows(i)], pages_ref.at[slot_rows(x_from * 2 + z_hi)],
            x_ss.at[i], x_rs.at[x_from], (seq, i * 2 + z_hi),
        )

    for i in range(xs):
        mid_copy(i).start()
    for i in range(1, xs):
        x_copy(lax.rem(x + i, xs), x).start()
    own_pages = pltpu.make_async_copy(
        pages_out.at[slot_rows(x)], pages_ref.at[slot_rows(rep)], local_sem.at[0]
    )
    own_pages.start()

    def rotate_queries(d):
        first = d * wide
        for j in range(heads):
            columns = pl.ds(pl.multiple_of(first + j * HEAD, HEAD), HEAD)
            q_out[d, :, j * HEAD:(j + 1) * HEAD] = rotate(q_ref[:, columns])

    def q_copy(d, row_of):
        return remote(
            q_out.at[d], q_mine.at[pl.ds(pl.multiple_of(row_of * tokens, tokens), tokens)],
            q_ss.at[d], q_rs.at[row_of], peer(d),
        )

    def send_queries(i, carry):
        d = lax.rem(g + i, groups)
        rotate_queries(d)
        q_copy(d, g).start()
        return carry

    lax.fori_loop(1, groups, send_queries, 0)
    rotate_queries(g)
    q_mine[my_rows, :] = q_out[g]

    def z_copy(block, part):
        part_rows = kv_all.at[block, pl.ds(part * half, half)]
        at = block * 2 + part
        return remote(part_rows, part_rows, z_ss.at[at], z_rs.at[at], (seq + groups, rep))

    for i in range(1, groups):
        d = lax.rem(g + i, groups)
        kv_copy(d, d).wait_recv()

    @pl.when(z < zs - 1)
    def _():
        for part in range(2):
            z_copy(z, part).start()

    for i in range(1, groups):
        d = lax.rem(g + i, groups)
        q_copy(d, d).wait_recv()

    def attend(block, diagonal):
        chunk = half
        for j in range(heads):
            for c in range(2):
                at = pl.ds(c * chunk, chunk)
                seen = (c + 1) * chunk if diagonal else rows
                keys = kv_all[block, 0:seen, 0:HEAD]
                values = kv_all[block, 0:seen, HEAD:2 * HEAD]
                scores = lax.dot_general(
                    q_mine[at, j * HEAD:(j + 1) * HEAD], keys, NT,
                    preferred_element_type=jnp.float32,
                )
                if diagonal:
                    query_at = lax.broadcasted_iota(jnp.int32, (chunk, seen), 0) + c * chunk
                    key_at = lax.broadcasted_iota(jnp.int32, (chunk, seen), 1)
                    scores = jnp.where(key_at <= query_at, scores, -1e30)
                largest = jnp.max(scores, axis=1, keepdims=True)
                if diagonal:
                    largest = jnp.broadcast_to(largest, (chunk, HEAD))
                else:
                    before = top[j, at, :]
                    largest = jnp.maximum(before, largest)
                    shrink = jnp.exp2((before - largest) * SCALE)
                top[j, at, :] = largest
                shift = jnp.concatenate([largest * SCALE] * max(1, seen // HEAD), axis=1)[:, :seen]
                weights = jnp.exp2(scores * SCALE - shift).astype(jnp.bfloat16)
                extended = jnp.concatenate([values, jnp.ones((seen, HEAD), jnp.bfloat16)], axis=1)
                result = jnp.dot(weights, extended, preferred_element_type=jnp.float32)
                if not diagonal:
                    result = acc[j, at, :] * jnp.concatenate([shrink, shrink], axis=1) + result
                acc[j, at, :] = result

    attend(z, True)

    def step(t, carry):
        @pl.when(t <= z)
        def _():
            block = z - t
            for part in range(2):
                z_copy(block, part).wait_recv()

                @pl.when(z < zs - 1)
                def _():
                    z_copy(block, part).start()
            attend(block, False)

        @pl.when(t <= xs)
        def _():
            mid_copy(t - 1).wait_recv()
            far_copy(t - 1, x).start()
        return carry

    lax.fori_loop(1, max(zs, xs + 1), step, 0)

    def o_copy(d, group_of):
        return remote(
            o_mine.at[pl.ds(pl.multiple_of(d * tokens, tokens), tokens)],
            o_ref.at[:, pl.ds(pl.multiple_of(group_of * wide, wide), wide)],
            o_ss.at[d], o_rs.at[group_of], peer(d),
        )

    def finish(d):
        at = pl.ds(pl.multiple_of(d * tokens, tokens), tokens)
        token = (z * groups + d) * tokens + lax.broadcasted_iota(jnp.int32, (tokens, HEAD), 0)
        for j in range(heads):
            total = acc[j, at, :]
            result = total[:, 0:HEAD] / total[:, HEAD:2 * HEAD]
            o_mine[at, j * HEAD:(j + 1) * HEAD] = jnp.where(token < length, result, 0.0).astype(
                jnp.bfloat16
            )

    def return_rows(i, carry):
        d = lax.rem(g + i, groups)
        finish(d)
        o_copy(d, g).start()
        return carry

    lax.fori_loop(1, groups, return_rows, 0)
    finish(g)
    own_rows = pltpu.make_async_copy(
        o_mine.at[my_rows], o_ref.at[:, pl.ds(pl.multiple_of(g * wide, wide), wide)],
        local_sem.at[1],
    )
    own_rows.start()

    for i in range(1, groups):
        d = lax.rem(g + i, groups)
        kv_copy(d, g).wait_send()
        q_copy(d, g).wait_send()
    for i in range(1, xs):
        other = lax.rem(x + i, xs)
        x_copy(other, x).wait_send()
        x_copy(other, other).wait_recv()
    for i in range(xs):
        mid_copy(i).wait_send()

    @pl.when(z < zs - 1)
    def _():
        def sent(block, carry):
            for part in range(2):
                z_copy(block, part).wait_send()
            return carry

        lax.fori_loop(0, z + 1, sent, 0)

    own_pages.wait()
    own_rows.wait()
    for i in range(1, groups):
        d = lax.rem(g + i, groups)
        o_copy(d, g).wait_send()
        o_copy(d, d).wait_recv()
    for i in range(xs):
        far_copy(i, x).wait_send()
        far_copy(i, i).wait_recv()


def body(query_rows, unrotated_keys, value_projections, lengths, page_table):
    tokens, query_width = query_rows.shape[1:]
    groups = unrotated_keys.shape[2] // HEAD
    zs = lax.axis_size("seq") // groups
    owners = lax.axis_size("rep")
    xs = owners // Z_HALVES
    rows, wide = groups * tokens, query_width // groups
    heads = wide // HEAD
    positions = lax.axis_index("seq") * tokens + jnp.arange(tokens, dtype=jnp.int32)
    cosine, sine = rotary_tables(positions)
    bf16, f32 = jnp.bfloat16, jnp.float32
    vmem = pl.BlockSpec(memory_space=pltpu.VMEM)
    smem = pl.BlockSpec(memory_space=pltpu.SMEM)
    dma = pltpu.SemaphoreType.DMA
    attended, pages = pl.pallas_call(
        functools.partial(kernel, groups, zs, xs),
        out_shape=(
            jax.ShapeDtypeStruct((tokens, query_width), bf16),
            jax.ShapeDtypeStruct((owners * SLOT_ROWS, 2 * groups * HEAD), bf16),
        ),
        in_specs=[vmem] * 5 + [smem] * 2,
        out_specs=(pl.BlockSpec(memory_space=pl.ANY),) * 2,
        scratch_shapes=[
            pltpu.VMEM((groups, tokens, 2 * HEAD), bf16),
            pltpu.VMEM((zs, rows, 2 * HEAD), bf16),
            pltpu.VMEM((groups, tokens, wide), bf16),
            pltpu.VMEM((rows, wide), bf16),
            pltpu.VMEM((rows, wide), bf16),
            pltpu.VMEM((heads, rows, 2 * HEAD), f32),
            pltpu.VMEM((heads, rows, HEAD), f32),
            pltpu.VMEM((owners * SLOT_ROWS, 2 * groups * HEAD), bf16),
            pltpu.VMEM((xs * SLOT_ROWS, 2 * groups * HEAD), bf16),
            dma((groups,)), dma((groups,)), dma((groups,)), dma((groups,)),
            dma((groups,)), dma((groups,)), dma((2 * zs,)), dma((2 * zs,)),
            dma((xs,)), dma((xs,)), dma((xs,)), dma((xs,)), dma((xs,)), dma((xs,)),
            dma((2,)),
        ],
        compiler_params=pltpu.CompilerParams(
            collective_id=0, has_side_effects=True, vmem_limit_bytes=48 * 2**20
        ),
        name="recompute",
    )(
        query_rows[0], unrotated_keys[0], value_projections[0], cosine, sine, lengths,
        page_table[0, :, 0],
    )
    return (
        attended[None],
        pages.reshape(1, 1, owners, SLOTS, PAGE, 2 * groups * HEAD),
    )


def solution(mesh):
    return jax.shard_map(
        body,
        mesh=mesh,
        in_specs=(
            P("rep", "seq", None),
            P("rep", "seq", None),
            P("rep", "seq", None),
            P("rep"),
            P("rep", "seq", None),
        ),
        out_specs=(P("rep", "seq", None), P("rep", "seq", None, None, None, None)),
        check_vma=False,
    )
```

time: 427 us -> 85.4 us (0.20); the launches traced: 420 us -> 85.2 us
  waiting for transfers between devices: 172 us -> 0 us
  matrix products: 105 us -> 0 us
  Pallas kernels: 0 us -> 79.9 us
  starting transfers between devices: 55.1 us -> 0 us
  other arithmetic: 55.3 us -> 0.29 us
  local copies, waits for them, and re-layouts: 19.3 us -> 3.68 us
  loops' own time: 11.4 us -> 0 us
    all_to_all x4 -> x0, waiting for transfers between devices: 172 us -> none  [the longest x1 87.1 us: body(): lax.all_to_all(widened, 'seq', split_axis=1, concat_axis=0, tiled=True)]
    dot_general x73 -> x0, matrix products: 105 us -> none  [the longest x36 56.8 us: key_step(): jnp.einsum('hqk,kd->hqd', weights.astype(jnp.bfloat16), value_part[:, 0],...]
    pallas_call x0 -> x1, Pallas kernels: none -> 79.9 us  [body(): pl.pallas_call(functools.partial(kernel, groups, zs, xs), out_shape=(jax....]
    all_to_all x4 -> x0, starting transfers between devices: 55.1 us -> none  [the longest x1 14 us: body(): lax.all_to_all(attended_heads, 'seq', split_axis=0, concat_axis=1, tiled=...]
    lt x45 -> x0, other arithmetic: 28.7 us -> none  [the longest x36 23.5 us: key_step(): key_positions[None, :] < length]
    reduce_sum x36 -> x0, other arithmetic: 12.8 us -> none  [key_step(): new_sum = running_sum * rescale + jnp.sum(weights, axis=-1)]
    another operation x9 -> x0, loops' own time: 11.4 us -> none  [the longest x1 9.35 us: attend_heads(): lax.map(query_block, jnp.arange(total_rows // block_rows, dtype=jnp.int32))]
    dynamic_update_slice x8 -> x0, other arithmetic: 6.93 us -> none  [attend_heads(): lax.map(query_block, jnp.arange(total_rows // block_rows, dtype=jnp.int32))]
  transfers between devices with their start and end apart: 4 -> 0, of which waited for: 3 -> 0; matrix products, arithmetic and copies ran while one was open for 41% -> 0% of each run, Pallas kernels for 0% -> 0%
where the time goes in v1:
time: 85.4 us; the launch traced here: 85.2 us
  Pallas kernels  79.9 us (94%)
  local copies, waits for them, and re-layouts  3.68 us (4%)
  between operations  1.34 us (2%)
    pallas_call x1, Pallas kernels, body(): pl.pallas_call(functools.partial(kernel, groups, zs, xs), out_shape=(jax....  79.9 us
    unnamed x10, local copies, waits for them, and re-layouts  3.68 us

profile of v1, /device:TPU:481, one launch (start us, length us, event | category | flops | bytes accessed | tf_op | source)
XLA Modules:
  0.0 85.2 jit_solution(2472482543652399421)
XLA Ops:
  1.3 0.0 copy-start.1
  1.3 0.0 copy-start.2
  1.3 0.2 fusion
  1.5 0.1 pad_maximum_fusion
  1.6 0.0 copy-start.3
  1.6 0.6 copy-done.1
  2.2 0.1 copy-done.2
  2.3 0.0 copy-done.3
  2.3 0.0 copy-start
  2.3 1.2 %copy-done = bf16[1,64,8192]{2,1,0:T(8,128)(2,1)S(1)} copy-done((bf16[1,64,8192]{2,1,0:T(8,128)(2,1)S(1)}, bf16[1,64,8192]{2,1,0:T(8,128)(2,1)}, u32[]{:S(2)}) %copy-start) | copy-done | bytes 1048600
  3.5 79.9 %recompute.1 = (bf16[64,8192]{1,0:T(8,128)(2,1)S(1)}, bf16[128,2048]{1,0:T(8,128)(2,1)S(1)}) custom-call(bf16[64,8192]{1,0:T(8,128)(2,1)S(1)} %bitcast.6, bf16[64,1024]{1,0:T(8,128)(2,1)S(1)} %bitcast.9, bf16[64,1024]{1,0:T(8,128)(2,1)S(1)} %bitcast.10, f32[64,128]{1,0:T(8,128)S(1)} %get-tuple-element.9.cos_ref, f32[64,128]{1,0:T(8,128)S(1)} %get-tuple-element.10.sin_ref, ...), custom_call_target="tpu_custom_call" | custom-call | tf_op jit(solution)/shard_map/recompute/pallas_call | solution.py:334
  83.4 1.0 %copy.10 = bf16[1,64,8192]{2,1,0:T(8,128)(2,1)} copy(bf16[1,64,8192]{2,1,0:T(8,128)(2,1)S(1)} %bitcast.7) | data formatting | bytes 2097152
  84.4 0.8 copy.11
  (2 shorter events, 0.0 us)
Async XLA Ops:
  1.3 0.9 %copy-start.1 = (bf16[1,64,1024]{2,1,0:T(8,128)(2,1)S(1)}, bf16[1,64,1024]{2,1,0:T(8,128)(2,1)}, u32[]{:S(2)}) copy-start(bf16[1,64,1024]{2,1,0:T(8,128)(2,1)} %param.6) | copy-start | bytes 393220
  1.3 1.0 %copy-start.2 = (bf16[1,64,1024]{2,1,0:T(8,128)(2,1)S(1)}, bf16[1,64,1024]{2,1,0:T(8,128)(2,1)}, u32[]{:S(2)}) copy-start(bf16[1,64,1024]{2,1,0:T(8,128)(2,1)} %param.7) | copy-start | bytes 393220
  1.6 0.7 copy-start.3
  2.3 1.2 %copy-start = (bf16[1,64,8192]{2,1,0:T(8,128)(2,1)S(1)}, bf16[1,64,8192]{2,1,0:T(8,128)(2,1)}, u32[]{:S(2)}) copy-start(bf16[1,64,8192]{2,1,0:T(8,128)(2,1)} %param.5) | copy-start | bytes 3145732

commit v2 on v1

v2 whole, which is shorter than its diff:
```python
import functools
import math

import jax
import jax.numpy as jnp
from jax import lax
from jax.experimental import pallas as pl
from jax.experimental.pallas import tpu as pltpu
from jax.sharding import PartitionSpec as P

HEAD = 128
PAGE = 8
SLOTS = 2
LEAD = 4
CATCH_UP = (8, 14, 20)
PAGE_STEPS = (7, 13, 18, 23)
SLOT_ROWS = SLOTS * PAGE
Z_HALVES = 2
SCALE = math.log2(math.e) / math.sqrt(HEAD)
MESH = pl.DeviceIdType.MESH
NT = (((1,), (1,)), ((), ()))


def rotary_tables(token_positions):
    halfwidth = HEAD // 2
    frequency = jnp.exp(
        -jnp.arange(halfwidth, dtype=jnp.float32) * (2.0 * math.log(500000.0) / HEAD)
    )
    angles = token_positions.astype(jnp.float32)[:, None] * frequency[None, :]
    cosine, sine = jnp.cos(angles), jnp.sin(angles)
    return (
        jnp.concatenate([cosine, cosine], axis=-1),
        jnp.concatenate([-sine, sine], axis=-1),
    )


def kernel(
    groups, zs, xs,
    q_ref, k_ref, v_ref, cos_ref, sin_ref, len_ref, table_ref,
    o_ref, pages_ref,
    kv_out, kv_all, q_out, q_mine, o_mine, acc, top, pages_out, pages_mid,
    kv_ss, kv_rs, q_ss, q_rs, o_ss, o_rs, z_ss, z_rs, sib_ss, sib_rs, x_ss, x_rs,
    mid_ss, mid_rs, far_ss, far_rs, local_sem,
):
    tokens = q_ref.shape[0]
    rows = groups * tokens
    heads = q_ref.shape[1] // (2 * groups * HEAD)
    wide = heads * HEAD
    half = rows // 2
    quarter = rows // 4
    quarter_shards = groups // 4
    ys = groups // 2
    span = 2 * zs
    hop = zs // 2
    seq, rep = lax.axis_index("seq"), lax.axis_index("rep")
    z, g = seq // groups, lax.rem(seq, groups)
    y, core = g // 2, lax.rem(g, 2)
    my_core = lax.rem(g // quarter_shards, 2)
    x, z_hi = rep // 2, lax.rem(rep, 2)
    z_abs = z_hi * zs + z
    units = z + 1

    def peer(d):
        return (z * groups + d, rep)

    def along_z(shift, x_at):
        to = lax.rem(z_abs + shift + span, span)
        return (lax.rem(to, zs) * groups + g, x_at * 2 + to // zs)

    def remote(src, dst, ss, rs, device):
        return pltpu.make_async_remote_copy(
            src_ref=src, dst_ref=dst, send_sem=ss, recv_sem=rs,
            device_id=device, device_id_type=MESH,
        )

    def token_rows(d):
        return pl.ds(pl.multiple_of(d * tokens, tokens), tokens)

    barrier = pltpu.get_barrier_semaphore()

    def greet(device):
        pl.semaphore_signal(barrier, inc=1, device_id=device, device_id_type=MESH)

    for i in range(1, groups):
        greet(peer(lax.rem(g + i, groups)))
    for i in range(1, xs):
        greet((seq, lax.rem(x + i, xs) * 2 + z_hi))
    for i in range(xs):
        greet(along_z(hop, i))

    @pl.when(z > 0)
    def _():
        greet((seq - groups, rep))

    cosine, sine = cos_ref[...], sin_ref[...]

    def rotate(head):
        head = head.astype(jnp.float32)
        return (head * cosine + pltpu.roll(head, HEAD // 2, axis=1) * sine).astype(jnp.bfloat16)

    for d in range(groups):
        kv_out[d, :, 0:HEAD] = rotate(k_ref[:, d * HEAD:(d + 1) * HEAD])
        kv_out[d, :, HEAD:2 * HEAD] = v_ref[:, d * HEAD:(d + 1) * HEAD]

    @pl.when(my_core == core)
    def _():
        for p in range(2):
            kv_all[p, z, token_rows(g), :] = kv_out[2 * y + p]

    length = len_ref[0]
    owners = [table_ref[j] for j in range(tokens // PAGE)]
    lane = lax.broadcasted_iota(jnp.int32, (1, tokens), 1)
    target = jnp.full((1, tokens), -1, jnp.int32)
    for j, owner in enumerate(owners):
        earlier = jnp.int32(0)
        for i in range(j):
            earlier = earlier + jnp.where(owners[i] == owner, 1, 0)
        owner_x = owner >> 1
        other = jnp.where((owner & 1) == z_hi, 0, xs)
        base = (other + owner_x) * SLOT_ROWS + earlier * PAGE - j * PAGE
        target = jnp.where(
            (lane >= j * PAGE) & (lane < (j + 1) * PAGE) & (earlier < SLOTS), lane + base, target
        )
    target = jnp.where(seq * tokens + lane < length, target, -1)
    slot = lax.broadcasted_iota(jnp.int32, (2 * xs * SLOT_ROWS, tokens), 0)
    chosen = jnp.where(slot == target, 1.0, 0.0).astype(jnp.bfloat16)
    for d in range(groups):
        for part in range(2):
            column = (part * groups + d) * HEAD
            pages_out[:, column:column + HEAD] = jnp.dot(
                chosen, kv_out[d, :, part * HEAD:(part + 1) * HEAD],
                preferred_element_type=jnp.float32,
            ).astype(jnp.bfloat16)

    def rotate_queries(p, d):
        first = ((d // 2 * 2 + p) * 2 + lax.rem(d, 2)) * wide
        for j in range(heads):
            columns = pl.ds(pl.multiple_of(first + j * HEAD, HEAD), HEAD)
            q_out[p, d, :, j * HEAD:(j + 1) * HEAD] = rotate(q_ref[:, columns])

    for p in range(2):
        def one(d, carry):
            rotate_queries(p, d)
            return carry

        lax.fori_loop(0, groups, one, 0)
        q_mine[p, token_rows(g), :] = q_out[p, g]

    partners = (groups - 1) + (xs - 1) + xs
    pl.semaphore_wait(barrier, partners + jnp.where(z < zs - 1, 1, 0))

    def kv_copy(p, y_to, row_of):
        return remote(
            kv_out.at[2 * y_to + p], kv_all.at[p, z, token_rows(row_of)],
            kv_ss.at[p * ys + y_to], kv_rs.at[p * groups + row_of],
            peer(2 * y_to + lax.rem(row_of // quarter_shards, 2)),
        )

    def each_kv_send(act):
        for p in range(2):
            for i in range(1, ys):
                act(kv_copy(p, lax.rem(y + i, ys), g))

            @pl.when(my_core != core)
            def _():
                act(kv_copy(p, y, g))

    each_kv_send(lambda copy: copy.start())

    def place(n):
        late = n >= 3 * units
        t = jnp.where(late, n - 3 * units, n // 3)
        kind = jnp.where(late, 3, n - 3 * t)
        return kind // 2, z - t, lax.rem(kind, 2)

    def quarter_of(p, block, piece, part):
        first = (piece * 2 + part) * quarter
        return kv_all.at[p, block, pl.ds(pl.multiple_of(first, quarter), quarter)]

    def z_copy(p, block, piece):
        at = (p * zs + block) * 2 + piece
        view = quarter_of(p, block, piece, core)
        return remote(view, view, z_ss.at[at], z_rs.at[at], (seq + groups, rep))

    def sib_copy(p, block, piece, part):
        at = (p * zs + block) * 2 + piece
        view = quarter_of(p, block, piece, part)
        return remote(view, view, sib_ss.at[at], sib_rs.at[at], peer(2 * y + 1 - core))

    def forward(n):
        p, block, piece = place(n)

        @pl.when(block == z)
        def _():
            for i in range(quarter_shards):
                source = (piece * 2 + core) * quarter_shards + i

                @pl.when(source != g)
                def _():
                    kv_copy(p, y, source).wait_recv()

        @pl.when(block != z)
        def _():
            z_copy(p, block, piece).wait_recv()

        @pl.when(z < zs - 1)
        def _():
            z_copy(p, block, piece).start()

        sib_copy(p, block, piece, core).start()

    def q_copy(p, d, row_of):
        return remote(
            q_out.at[p, d], q_mine.at[p, token_rows(row_of)],
            q_ss.at[p * groups + d], q_rs.at[p * groups + row_of], peer(d),
        )


    def slot_rows(i):
        return pl.ds(pl.multiple_of(i * SLOT_ROWS, SLOT_ROWS), SLOT_ROWS)

    def mid_copy(i):
        return remote(
            pages_out.at[slot_rows(xs + i)], pages_mid.at[slot_rows(i)],
            mid_ss.at[i], mid_rs.at[i], along_z(-hop, x),
        )

    def far_copy(i, x_from):
        origin = lax.rem(z_abs + hop, span)
        return remote(
            pages_mid.at[slot_rows(i)], pages_ref.at[slot_rows(x_from * 2 + origin // zs)],
            far_ss.at[i], far_rs.at[x_from], along_z(-hop, i),
        )

    def x_copy(i, x_from):
        return remote(
            pages_out.at[slot_rows(i)], pages_ref.at[slot_rows(x_from * 2 + z_hi)],
            x_ss.at[i], x_rs.at[x_from], (seq, i * 2 + z_hi),
        )

    def pass_pages(i):
        mid_copy(i).wait_recv()
        far_copy(i, x).start()

    for i in range(xs):
        mid_copy(i).start()
    for i in range(1, groups):
        q_copy(0, lax.rem(g + i, groups), g).start()
    forward(0)
    for i in range(1, xs):
        x_copy(lax.rem(x + i, xs), x).start()
    own_pages = pltpu.make_async_copy(
        pages_out.at[slot_rows(x)], pages_ref.at[slot_rows(rep)], local_sem.at[0]
    )
    own_pages.start()
    forward(1)
    for i in range(1, groups):
        q_copy(1, lax.rem(g + i, groups), g).start()
    for n in range(2, 4):
        forward(n)

    @pl.when(units > 1)
    def _():
        forward(4)

    def attend(p, block, piece, chunks, diagonal, first):
        keys_at = pl.ds(piece * half, half) if isinstance(piece, int) else pl.ds(
            pl.multiple_of(piece * half, half), half
        )
        keys = kv_all[p, block, keys_at, 0:HEAD]
        values = kv_all[p, block, keys_at, HEAD:2 * HEAD]
        extended = jnp.concatenate([values, jnp.ones((half, HEAD), jnp.bfloat16)], axis=1)
        for j in range(heads):
            for c in chunks:
                at = pl.ds(c * half, half)
                scores = lax.dot_general(
                    q_mine[p, at, j * HEAD:(j + 1) * HEAD], keys, NT,
                    preferred_element_type=jnp.float32,
                )
                if c == diagonal:
                    query_at = lax.broadcasted_iota(jnp.int32, (half, half), 0)
                    key_at = lax.broadcasted_iota(jnp.int32, (half, half), 1)
                    scores = jnp.where(key_at <= query_at, scores, -1e30)
                largest = jnp.max(scores, axis=1, keepdims=True)
                if first:
                    largest = jnp.broadcast_to(largest, (half, HEAD))
                else:
                    before = top[p, j, at, :]
                    largest = jnp.maximum(before, largest)
                    shrink = jnp.exp2((before - largest) * SCALE)
                top[p, j, at, :] = largest
                shift = jnp.concatenate([largest * SCALE] * max(1, half // HEAD), axis=1)[:, :half]
                weights = jnp.exp2(scores * SCALE - shift).astype(jnp.bfloat16)
                result = jnp.dot(weights, extended, preferred_element_type=jnp.float32)
                if not first:
                    result = acc[p, j, at, :] * jnp.concatenate([shrink, shrink], axis=1) + result
                acc[p, j, at, :] = result

    def o_columns(p, d):
        first = ((d // 2 * 2 + p) * 2 + lax.rem(d, 2)) * wide
        return o_ref.at[:, pl.ds(pl.multiple_of(first, wide), wide)]

    def o_copy(p, d, group_of):
        return remote(
            o_mine.at[p, token_rows(d)], o_columns(p, group_of),
            o_ss.at[p * groups + d], o_rs.at[p * groups + group_of], peer(d),
        )

    def own_rows(p):
        return pltpu.make_async_copy(
            o_mine.at[p, token_rows(g)], o_columns(p, g), local_sem.at[1 + p]
        )

    def finish(p, d):
        token = (z * groups + d) * tokens + lax.broadcasted_iota(jnp.int32, (tokens, HEAD), 0)
        for j in range(heads):
            total = acc[p, j, token_rows(d), :]
            result = total[:, 0:HEAD] / total[:, HEAD:2 * HEAD]
            o_mine[p, token_rows(d), j * HEAD:(j + 1) * HEAD] = jnp.where(
                token < length, result, 0.0
            ).astype(jnp.bfloat16)

    def step(i, carry):
        ahead = i + LEAD
        fresh = i >= 1
        for at in CATCH_UP:
            ahead = ahead - jnp.where(i >= at, 1, 0)
            fresh = fresh & (i != at)

        @pl.when(fresh & (ahead < 4 * units))
        def _():
            forward(ahead)

        moved = jnp.where(i == 4, 2, jnp.where((i == 2) | (i == 3), i + 1, i))
        n = jnp.where(units > 1, moved, i)
        p, block, piece = place(n)
        sib_copy(p, block, piece, 1 - core).wait_recv()

        @pl.when((block == z) & (piece == 0))
        def _():
            for d in range(1, groups):
                source = lax.rem(g + d, groups)
                q_copy(p, source, source).wait_recv()
            attend(p, block, 0, (0, 1), 0, True)

        @pl.when((block == z) & (piece == 1))
        def _():
            attend(p, block, 1, (1,), 1, False)

        @pl.when(block != z)
        def _():
            attend(p, block, piece, (0, 1), None, False)

        @pl.when((block == 0) & (piece == 1))
        def _():
            def return_rows(i, carry):
                d = lax.rem(g + i, groups)
                finish(p, d)
                o_copy(p, d, g).start()
                return carry

            lax.fori_loop(1, groups, return_rows, 0)
            finish(p, g)
            own_rows(p).start()

        for part in range(xs):
            @pl.when(i == PAGE_STEPS[part])
            def _():
                pass_pages(part)

        return carry

    lax.fori_loop(0, 4 * units, step, 0)

    for i in range(xs):
        @pl.when(PAGE_STEPS[i] >= 4 * units)
        def _():
            pass_pages(i)

    each_kv_send(lambda copy: copy.wait_send())
    for p in range(2):
        for i in range(1, groups):
            q_copy(p, lax.rem(g + i, groups), g).wait_send()
    for i in range(1, xs):
        other = lax.rem(x + i, xs)
        x_copy(other, x).wait_send()
        x_copy(other, other).wait_recv()
    for i in range(xs):
        mid_copy(i).wait_send()

    def sent(n, carry):
        p, block, piece = place(n)
        sib_copy(p, block, piece, core).wait_send()

        @pl.when(z < zs - 1)
        def _():
            z_copy(p, block, piece).wait_send()

        return carry

    lax.fori_loop(0, 4 * units, sent, 0)
    own_pages.wait()
    for p in range(2):
        own_rows(p).wait()
        for i in range(1, groups):
            d = lax.rem(g + i, groups)
            o_copy(p, d, g).wait_send()
            o_copy(p, d, d).wait_recv()
    for i in range(xs):
        far_copy(i, x).wait_send()
        far_copy(i, i).wait_recv()


def body(query_rows, unrotated_keys, value_projections, lengths, page_table):
    tokens, query_width = query_rows.shape[1:]
    groups = unrotated_keys.shape[2] // HEAD
    zs = lax.axis_size("seq") // groups
    owners = lax.axis_size("rep")
    xs = owners // Z_HALVES
    rows, wide = groups * tokens, query_width // (2 * groups)
    heads = wide // HEAD
    positions = lax.axis_index("seq") * tokens + jnp.arange(tokens, dtype=jnp.int32)
    cosine, sine = rotary_tables(positions)
    bf16, f32 = jnp.bfloat16, jnp.float32
    vmem = pl.BlockSpec(memory_space=pltpu.VMEM)
    smem = pl.BlockSpec(memory_space=pltpu.SMEM)
    dma = pltpu.SemaphoreType.DMA
    attended, pages = pl.pallas_call(
        functools.partial(kernel, groups, zs, xs),
        out_shape=(
            jax.ShapeDtypeStruct((tokens, query_width), bf16),
            jax.ShapeDtypeStruct((owners * SLOT_ROWS, 2 * groups * HEAD), bf16),
        ),
        in_specs=[vmem] * 5 + [smem] * 2,
        out_specs=(pl.BlockSpec(memory_space=pl.ANY),) * 2,
        scratch_shapes=[
            pltpu.VMEM((groups, tokens, 2 * HEAD), bf16),
            pltpu.VMEM((2, zs, rows, 2 * HEAD), bf16),
            pltpu.VMEM((2, groups, tokens, wide), bf16),
            pltpu.VMEM((2, rows, wide), bf16),
            pltpu.VMEM((2, rows, wide), bf16),
            pltpu.VMEM((2, heads, rows, 2 * HEAD), f32),
            pltpu.VMEM((2, heads, rows, HEAD), f32),
            pltpu.VMEM((owners * SLOT_ROWS, 2 * groups * HEAD), bf16),
            pltpu.VMEM((xs * SLOT_ROWS, 2 * groups * HEAD), bf16),
            dma((groups,)), dma((2 * groups,)), dma((2 * groups,)), dma((2 * groups,)),
            dma((2 * groups,)), dma((2 * groups,)), dma((4 * zs,)), dma((4 * zs,)),
            dma((4 * zs,)), dma((4 * zs,)),
            dma((xs,)), dma((xs,)), dma((xs,)), dma((xs,)), dma((xs,)), dma((xs,)),
            dma((3,)),
        ],
        compiler_params=pltpu.CompilerParams(
            collective_id=0, has_side_effects=True, vmem_limit_bytes=48 * 2**20
        ),
        name="recompute",
    )(
        query_rows[0], unrotated_keys[0], value_projections[0], cosine, sine, lengths,
        page_table[0, :, 0],
    )
    return (
        attended[None],
        pages.reshape(1, 1, owners, SLOTS, PAGE, 2 * groups * HEAD),
    )


def solution(mesh):
    return jax.shard_map(
        body,
        mesh=mesh,
        in_specs=(
            P("rep", "seq", None),
            P("rep", "seq", None),
            P("rep", "seq", None),
            P("rep"),
            P("rep", "seq", None),
        ),
        out_specs=(P("rep", "seq", None), P("rep", "seq", None, None, None, None)),
        check_vma=False,
    )
```

time: 85.4 us -> 75.5 us (0.88)
  the two profiles are of different devices: /device:TPU:481 before, /device:TPU:7 now
where the time goes in v2:
time: 75.5 us; the launch traced here: 75.3 us
  Pallas kernels  70 us (93%)
  local copies, waits for them, and re-layouts  3.68 us (5%)
  between operations  1.34 us (2%)
    pallas_call x1, Pallas kernels, body(): pl.pallas_call(functools.partial(kernel, groups, zs, xs), out_shape=(jax....  70 us
    unnamed x10, local copies, waits for them, and re-layouts  3.68 us

profile of v2, /device:TPU:7, one launch (start us, length us, event | category | flops | bytes accessed | tf_op | source)
XLA Modules:
  0.0 75.3 jit_solution(2696647820969883431)
XLA Ops:
  1.3 0.0 copy-start.1
  1.3 0.0 copy-start.2
  1.3 0.2 fusion
  1.5 0.1 pad_maximum_fusion
  1.6 0.0 copy-start.3
  1.6 0.6 copy-done.1
  2.2 0.1 copy-done.2
  2.3 0.0 copy-done.3
  2.3 0.0 copy-start
  2.3 1.2 %copy-done = bf16[1,64,8192]{2,1,0:T(8,128)(2,1)S(1)} copy-done((bf16[1,64,8192]{2,1,0:T(8,128)(2,1)S(1)}, bf16[1,64,8192]{2,1,0:T(8,128)(2,1)}, u32[]{:S(2)}) %copy-start) | copy-done | bytes 1048600
  3.5 70.0 %recompute.1 = (bf16[64,8192]{1,0:T(8,128)(2,1)S(1)}, bf16[128,2048]{1,0:T(8,128)(2,1)S(1)}) custom-call(bf16[64,8192]{1,0:T(8,128)(2,1)S(1)} %bitcast.6, bf16[64,1024]{1,0:T(8,128)(2,1)S(1)} %bitcast.9, bf16[64,1024]{1,0:T(8,128)(2,1)S(1)} %bitcast.10, f32[64,128]{1,0:T(8,128)S(1)} %get-tuple-element.9.cos_ref, f32[64,128]{1,0:T(8,128)S(1)} %get-tuple-element.10.sin_ref, ...), custom_call_target="tpu_custom_call" | custom-call | tf_op jit(solution)/shard_map/recompute/pallas_call | solution.py:428
  73.6 1.0 %copy.10 = bf16[1,64,8192]{2,1,0:T(8,128)(2,1)} copy(bf16[1,64,8192]{2,1,0:T(8,128)(2,1)S(1)} %bitcast.7) | data formatting | bytes 2097152
  74.5 0.8 %copy.11 = bf16[1,1,8,2,8,2048]{5,4,3,2,1,0:T(8,128)(2,1)} copy(bf16[1,1,8,2,8,2048]{5,4,3,2,1,0:T(8,128)(2,1)S(1)} %bitcast.8) | data formatting | bytes 1048576
  (2 shorter events, 0.0 us)
Async XLA Ops:
  1.3 0.9 %copy-start.1 = (bf16[1,64,1024]{2,1,0:T(8,128)(2,1)S(1)}, bf16[1,64,1024]{2,1,0:T(8,128)(2,1)}, u32[]{:S(2)}) copy-start(bf16[1,64,1024]{2,1,0:T(8,128)(2,1)} %param.6) | copy-start | bytes 393220
  1.3 1.0 %copy-start.2 = (bf16[1,64,1024]{2,1,0:T(8,128)(2,1)S(1)}, bf16[1,64,1024]{2,1,0:T(8,128)(2,1)}, u32[]{:S(2)}) copy-start(bf16[1,64,1024]{2,1,0:T(8,128)(2,1)} %param.7) | copy-start | bytes 393220
  1.6 0.7 copy-start.3
  2.3 1.2 %copy-start = (bf16[1,64,8192]{2,1,0:T(8,128)(2,1)S(1)}, bf16[1,64,8192]{2,1,0:T(8,128)(2,1)}, u32[]{:S(2)}) copy-start(bf16[1,64,8192]{2,1,0:T(8,128)(2,1)} %param.5) | copy-start | bytes 3145732

commit v3 on v2

--- a/solution.py
+++ b/solution.py
@@ -11,14 +11,25 @@
 HEAD = 128
 PAGE = 8
 SLOTS = 2
-LEAD = 4
-CATCH_UP = (8, 14, 20)
-PAGE_STEPS = (7, 13, 18, 23)
+LEAD = 6
+CATCH_UP = (5, 9, 13, 17, 21)
+ORDER_TWO = (0, 1, 3, 4, 2, 5)
+ORDER_MORE = (0, 1, 3, 4, 6, 7, 2, 5, 8)
+PAGE_STEPS = (6, 11, 15, 19)
 SLOT_ROWS = SLOTS * PAGE
 Z_HALVES = 2
 SCALE = math.log2(math.e) / math.sqrt(HEAD)
 MESH = pl.DeviceIdType.MESH
 NT = (((1,), (1,)), ((), ()))
+
+
+def both_ways(n):
+    first = [2, n - 2, 3, n - 1, n // 2, n // 2 + 1]
+    return list(dict.fromkeys([i for i in first if 1 < i < n] + list(range(n - 1, 0, -1))))
+
+
+def wrap(value, n):
+    return jnp.where(value >= n, value - n, value)
 
 
 def rotary_tables(token_positions):
@@ -50,22 +61,21 @@
     quarter = rows // 4
     quarter_shards = groups // 4
     ys = groups // 2
-    span = 2 * zs
     hop = zs // 2
     seq, rep = lax.axis_index("seq"), lax.axis_index("rep")
     z, g = seq // groups, lax.rem(seq, groups)
     y, core = g // 2, lax.rem(g, 2)
     my_core = lax.rem(g // quarter_shards, 2)
     x, z_hi = rep // 2, lax.rem(rep, 2)
-    z_abs = z_hi * zs + z
     units = z + 1
 
     def peer(d):
         return (z * groups + d, rep)
 
     def along_z(shift, x_at):
-        to = lax.rem(z_abs + shift + span, span)
-        return (lax.rem(to, zs) * groups + g, x_at * 2 + to // zs)
+        inside = (z + shift >= 0) & (z + shift < zs)
+        step = jnp.where(inside, shift, jnp.where(z + shift < 0, shift + zs, shift - zs))
+        return (seq + step * groups, x_at * 2 + jnp.where(inside, z_hi, 1 - z_hi))
 
     def remote(src, dst, ss, rs, device):
         return pltpu.make_async_remote_copy(
@@ -82,9 +92,9 @@
         pl.semaphore_signal(barrier, inc=1, device_id=device, device_id_type=MESH)
 
     for i in range(1, groups):
-        greet(peer(lax.rem(g + i, groups)))
+        greet(peer(wrap(g + i, groups)))
     for i in range(1, xs):
-        greet((seq, lax.rem(x + i, xs) * 2 + z_hi))
+        greet((seq, wrap(x + i, xs) * 2 + z_hi))
     for i in range(xs):
         greet(along_z(hop, i))
 
@@ -158,8 +168,8 @@
 
     def each_kv_send(act):
         for p in range(2):
-            for i in range(1, ys):
-                act(kv_copy(p, lax.rem(y + i, ys), g))
+            for i in sorted(range(1, ys), key=lambda i: abs(i - ys / 2), reverse=True):
+                act(kv_copy(p, wrap(y + i, ys), g))
 
             @pl.when(my_core != core)
             def _():
@@ -226,9 +236,9 @@
         )
 
     def far_copy(i, x_from):
-        origin = lax.rem(z_abs + hop, span)
-        return remote(
-            pages_mid.at[slot_rows(i)], pages_ref.at[slot_rows(x_from * 2 + origin // zs)],
+        origin_hi = jnp.where(z + hop < zs, z_hi, 1 - z_hi)
+        return remote(
+            pages_mid.at[slot_rows(i)], pages_ref.at[slot_rows(x_from * 2 + origin_hi)],
             far_ss.at[i], far_rs.at[x_from], along_z(-hop, i),
         )
 
@@ -244,24 +254,25 @@
 
     for i in range(xs):
         mid_copy(i).start()
-    for i in range(1, groups):
-        q_copy(0, lax.rem(g + i, groups), g).start()
+    for i in both_ways(groups):
+        q_copy(0, wrap(g + i, groups), g).start()
     forward(0)
     for i in range(1, xs):
-        x_copy(lax.rem(x + i, xs), x).start()
+        x_copy(wrap(x + i, xs), x).start()
     own_pages = pltpu.make_async_copy(
         pages_out.at[slot_rows(x)], pages_ref.at[slot_rows(rep)], local_sem.at[0]
     )
     own_pages.start()
     forward(1)
-    for i in range(1, groups):
-        q_copy(1, lax.rem(g + i, groups), g).start()
+    for i in both_ways(groups):
+        q_copy(1, wrap(g + i, groups), g).start()
     for n in range(2, 4):
         forward(n)
 
     @pl.when(units > 1)
     def _():
-        forward(4)
+        for n in range(4, LEAD + 1):
+            forward(n)
 
     def attend(p, block, piece, chunks, diagonal, first):
         keys_at = pl.ds(piece * half, half) if isinstance(piece, int) else pl.ds(
@@ -331,15 +342,17 @@
         def _():
             forward(ahead)
 
-        moved = jnp.where(i == 4, 2, jnp.where((i == 2) | (i == 3), i + 1, i))
-        n = jnp.where(units > 1, moved, i)
+        n = i
+        for known, order in ((units == 2, ORDER_TWO), (units > 2, ORDER_MORE)):
+            for at, index in enumerate(order):
+                n = jnp.where(known & (i == at), index, n)
         p, block, piece = place(n)
         sib_copy(p, block, piece, 1 - core).wait_recv()
 
         @pl.when((block == z) & (piece == 0))
         def _():
             for d in range(1, groups):
-                source = lax.rem(g + d, groups)
+                source = wrap(g + d, groups)
                 q_copy(p, source, source).wait_recv()
             attend(p, block, 0, (0, 1), 0, True)
 
@@ -353,13 +366,10 @@
 
         @pl.when((block == 0) & (piece == 1))
         def _():
-            def return_rows(i, carry):
-                d = lax.rem(g + i, groups)
+            for offset in both_ways(groups):
+                d = wrap(g + offset, groups)
                 finish(p, d)
                 o_copy(p, d, g).start()
-                return carry
-
-            lax.fori_loop(1, groups, return_rows, 0)
             finish(p, g)
             own_rows(p).start()
 
@@ -380,9 +390,9 @@
     each_kv_send(lambda copy: copy.wait_send())
     for p in range(2):
         for i in range(1, groups):
-            q_copy(p, lax.rem(g + i, groups), g).wait_send()
+            q_copy(p, wrap(g + i, groups), g).wait_send()
     for i in range(1, xs):
-        other = lax.rem(x + i, xs)
+        other = wrap(x + i, xs)
         x_copy(other, x).wait_send()
         x_copy(other, other).wait_recv()
     for i in range(xs):
@@ -403,7 +413,7 @@
     for p in range(2):
         own_rows(p).wait()
         for i in range(1, groups):
-            d = lax.rem(g + i, groups)
+            d = wrap(g + i, groups)
             o_copy(p, d, g).wait_send()
             o_copy(p, d, d).wait_recv()
     for i in range(xs):

time: 75.5 us -> 73.4 us (0.972)
  the two profiles are of different devices: /device:TPU:7 before, /device:TPU:481 now
where the time goes in v3:
time: 73.4 us; the launch traced here: 73.2 us
  Pallas kernels  67.9 us (93%)
  local copies, waits for them, and re-layouts  3.68 us (5%)
  between operations  1.34 us (2%)
    pallas_call x1, Pallas kernels, body(): pl.pallas_call(functools.partial(kernel, groups, zs, xs), out_shape=(jax....  67.9 us
    unnamed x10, local copies, waits for them, and re-layouts  3.68 us

profile of v3, /device:TPU:481, one launch (start us, length us, event | category | flops | bytes accessed | tf_op | source)
XLA Modules:
  0.0 73.2 jit_solution(10865833825938903119)
XLA Ops:
  1.3 0.0 copy-start.1
  1.3 0.0 copy-start.2
  1.3 0.2 fusion
  1.5 0.1 pad_maximum_fusion
  1.6 0.0 copy-start.3
  1.6 0.6 copy-done.1
  2.2 0.1 copy-done.2
  2.3 0.0 copy-done.3
  2.3 0.0 copy-start
  2.3 1.2 %copy-done = bf16[1,64,8192]{2,1,0:T(8,128)(2,1)S(1)} copy-done((bf16[1,64,8192]{2,1,0:T(8,128)(2,1)S(1)}, bf16[1,64,8192]{2,1,0:T(8,128)(2,1)}, u32[]{:S(2)}) %copy-start) | copy-done | bytes 1048600
  3.5 67.9 %recompute.1 = (bf16[64,8192]{1,0:T(8,128)(2,1)S(1)}, bf16[128,2048]{1,0:T(8,128)(2,1)S(1)}) custom-call(bf16[64,8192]{1,0:T(8,128)(2,1)S(1)} %bitcast.6, bf16[64,1024]{1,0:T(8,128)(2,1)S(1)} %bitcast.9, bf16[64,1024]{1,0:T(8,128)(2,1)S(1)} %bitcast.10, f32[64,128]{1,0:T(8,128)S(1)} %get-tuple-element.9.cos_ref, f32[64,128]{1,0:T(8,128)S(1)} %get-tuple-element.10.sin_ref, ...), custom_call_target="tpu_custom_call" | custom-call | tf_op jit(solution)/shard_map/recompute/pallas_call | solution.py:438
  71.4 1.0 %copy.10 = bf16[1,64,8192]{2,1,0:T(8,128)(2,1)} copy(bf16[1,64,8192]{2,1,0:T(8,128)(2,1)S(1)} %bitcast.7) | data formatting | bytes 2097152
  72.4 0.8 %copy.11 = bf16[1,1,8,2,8,2048]{5,4,3,2,1,0:T(8,128)(2,1)} copy(bf16[1,1,8,2,8,2048]{5,4,3,2,1,0:T(8,128)(2,1)S(1)} %bitcast.8) | data formatting | bytes 1048576
  (2 shorter events, 0.0 us)
Async XLA Ops:
  1.3 0.9 %copy-start.1 = (bf16[1,64,1024]{2,1,0:T(8,128)(2,1)S(1)}, bf16[1,64,1024]{2,1,0:T(8,128)(2,1)}, u32[]{:S(2)}) copy-start(bf16[1,64,1024]{2,1,0:T(8,128)(2,1)} %param.6) | copy-start | bytes 393220
  1.3 1.0 %copy-start.2 = (bf16[1,64,1024]{2,1,0:T(8,128)(2,1)S(1)}, bf16[1,64,1024]{2,1,0:T(8,128)(2,1)}, u32[]{:S(2)}) copy-start(bf16[1,64,1024]{2,1,0:T(8,128)(2,1)} %param.7) | copy-start | bytes 393220
  1.6 0.7 copy-start.3
  2.3 1.2 %copy-start = (bf16[1,64,8192]{2,1,0:T(8,128)(2,1)S(1)}, bf16[1,64,8192]{2,1,0:T(8,128)(2,1)}, u32[]{:S(2)}) copy-start(bf16[1,64,8192]{2,1,0:T(8,128)(2,1)} %param.5) | copy-start | bytes 3145732

commit v4 on v3

--- a/solution.py
+++ b/solution.py
@@ -15,7 +15,7 @@
 CATCH_UP = (5, 9, 13, 17, 21)
 ORDER_TWO = (0, 1, 3, 4, 2, 5)
 ORDER_MORE = (0, 1, 3, 4, 6, 7, 2, 5, 8)
-PAGE_STEPS = (6, 11, 15, 19)
+PAGE_STEPS = (5, 9, 13, 17)
 SLOT_ROWS = SLOTS * PAGE
 Z_HALVES = 2
 SCALE = math.log2(math.e) / math.sqrt(HEAD)
@@ -190,7 +190,8 @@
     def z_copy(p, block, piece):
         at = (p * zs + block) * 2 + piece
         view = quarter_of(p, block, piece, core)
-        return remote(view, view, z_ss.at[at], z_rs.at[at], (seq + groups, rep))
+        device = (jnp.where(z < zs - 1, seq + groups, seq - groups), rep)
+        return remote(view, view, z_ss.at[at], z_rs.at[at], device)
 
     def sib_copy(p, block, piece, part):
         at = (p * zs + block) * 2 + piece

time: 73.4 us -> 73.4 us (level)
  no operation moved by 1% of the time
where the time goes in v4:
time: 73.4 us; the launch traced here: 73.2 us
  Pallas kernels  67.9 us (93%)
  local copies, waits for them, and re-layouts  3.68 us (5%)
  between operations  1.34 us (2%)
    pallas_call x1, Pallas kernels, body(): pl.pallas_call(functools.partial(kernel, groups, zs, xs), out_shape=(jax....  67.9 us
    unnamed x10, local copies, waits for them, and re-layouts  3.68 us

profile of v4, /device:TPU:481, one launch (start us, length us, event | category | flops | bytes accessed | tf_op | source)
XLA Modules:
  0.0 73.2 jit_solution(5355677599699516048)
XLA Ops:
  1.3 0.0 copy-start.1
  1.3 0.0 copy-start.2
  1.3 0.2 fusion
  1.5 0.1 pad_maximum_fusion
  1.6 0.0 copy-start.3
  1.6 0.6 copy-done.1
  2.2 0.1 copy-done.2
  2.3 0.0 copy-done.3
  2.3 0.0 copy-start
  2.3 1.2 %copy-done = bf16[1,64,8192]{2,1,0:T(8,128)(2,1)S(1)} copy-done((bf16[1,64,8192]{2,1,0:T(8,128)(2,1)S(1)}, bf16[1,64,8192]{2,1,0:T(8,128)(2,1)}, u32[]{:S(2)}) %copy-start) | copy-done | bytes 1048600
  3.5 67.9 %recompute.1 = (bf16[64,8192]{1,0:T(8,128)(2,1)S(1)}, bf16[128,2048]{1,0:T(8,128)(2,1)S(1)}) custom-call(bf16[64,8192]{1,0:T(8,128)(2,1)S(1)} %bitcast.6, bf16[64,1024]{1,0:T(8,128)(2,1)S(1)} %bitcast.9, bf16[64,1024]{1,0:T(8,128)(2,1)S(1)} %bitcast.10, f32[64,128]{1,0:T(8,128)S(1)} %get-tuple-element.9.cos_ref, f32[64,128]{1,0:T(8,128)S(1)} %get-tuple-element.10.sin_ref, ...), custom_call_target="tpu_custom_call" | custom-call | tf_op jit(solution)/shard_map/recompute/pallas_call | solution.py:439
  71.4 1.0 %copy.10 = bf16[1,64,8192]{2,1,0:T(8,128)(2,1)} copy(bf16[1,64,8192]{2,1,0:T(8,128)(2,1)S(1)} %bitcast.7) | data formatting | bytes 2097152
  72.4 0.8 %copy.11 = bf16[1,1,8,2,8,2048]{5,4,3,2,1,0:T(8,128)(2,1)} copy(bf16[1,1,8,2,8,2048]{5,4,3,2,1,0:T(8,128)(2,1)S(1)} %bitcast.8) | data formatting | bytes 1048576
  (2 shorter events, 0.0 us)
Async XLA Ops:
  1.3 0.9 %copy-start.1 = (bf16[1,64,1024]{2,1,0:T(8,128)(2,1)S(1)}, bf16[1,64,1024]{2,1,0:T(8,128)(2,1)}, u32[]{:S(2)}) copy-start(bf16[1,64,1024]{2,1,0:T(8,128)(2,1)} %param.6) | copy-start | bytes 393220
  1.3 1.0 %copy-start.2 = (bf16[1,64,1024]{2,1,0:T(8,128)(2,1)S(1)}, bf16[1,64,1024]{2,1,0:T(8,128)(2,1)}, u32[]{:S(2)}) copy-start(bf16[1,64,1024]{2,1,0:T(8,128)(2,1)} %param.7) | copy-start | bytes 393220
  1.6 0.7 copy-start.3
  2.3 1.2 %copy-start = (bf16[1,64,8192]{2,1,0:T(8,128)(2,1)S(1)}, bf16[1,64,8192]{2,1,0:T(8,128)(2,1)}, u32[]{:S(2)}) copy-start(bf16[1,64,8192]{2,1,0:T(8,128)(2,1)} %param.5) | copy-start | bytes 3145732

commit v5 on v4

--- a/solution.py
+++ b/solution.py
@@ -91,12 +91,12 @@
     def greet(device):
         pl.semaphore_signal(barrier, inc=1, device_id=device, device_id_type=MESH)
 
+    for i in range(xs):
+        greet(along_z(hop, i))
+    for i in range(1, xs):
+        greet((seq, wrap(x + i, xs) * 2 + z_hi))
     for i in range(1, groups):
         greet(peer(wrap(g + i, groups)))
-    for i in range(1, xs):
-        greet((seq, wrap(x + i, xs) * 2 + z_hi))
-    for i in range(xs):
-        greet(along_z(hop, i))
 
     @pl.when(z > 0)
     def _():

time: 73.4 us -> 73.3 us (level)
  no operation moved by 1% of the time
where the time goes in v5:
time: 73.3 us; the launch traced here: 73.1 us
  Pallas kernels  67.8 us (92%)
  local copies, waits for them, and re-layouts  3.68 us (5%)
  between operations  1.34 us (2%)
    pallas_call x1, Pallas kernels, body(): pl.pallas_call(functools.partial(kernel, groups, zs, xs), out_shape=(jax....  67.8 us
    unnamed x10, local copies, waits for them, and re-layouts  3.68 us

profile of v5, /device:TPU:481, one launch (start us, length us, event | category | flops | bytes accessed | tf_op | source)
XLA Modules:
  0.0 73.1 jit_solution(1704436111759073454)
XLA Ops:
  1.3 0.0 copy-start.1
  1.3 0.0 copy-start.2
  1.3 0.2 fusion
  1.5 0.1 pad_maximum_fusion
  1.6 0.0 copy-start.3
  1.6 0.6 copy-done.1
  2.2 0.1 copy-done.2
  2.3 0.0 copy-done.3
  2.3 0.0 copy-start
  2.3 1.2 %copy-done = bf16[1,64,8192]{2,1,0:T(8,128)(2,1)S(1)} copy-done((bf16[1,64,8192]{2,1,0:T(8,128)(2,1)S(1)}, bf16[1,64,8192]{2,1,0:T(8,128)(2,1)}, u32[]{:S(2)}) %copy-start) | copy-done | bytes 1048600
  3.5 67.8 %recompute.1 = (bf16[64,8192]{1,0:T(8,128)(2,1)S(1)}, bf16[128,2048]{1,0:T(8,128)(2,1)S(1)}) custom-call(bf16[64,8192]{1,0:T(8,128)(2,1)S(1)} %bitcast.6, bf16[64,1024]{1,0:T(8,128)(2,1)S(1)} %bitcast.9, bf16[64,1024]{1,0:T(8,128)(2,1)S(1)} %bitcast.10, f32[64,128]{1,0:T(8,128)S(1)} %get-tuple-element.9.cos_ref, f32[64,128]{1,0:T(8,128)S(1)} %get-tuple-element.10.sin_ref, ...), custom_call_target="tpu_custom_call" | custom-call | tf_op jit(solution)/shard_map/recompute/pallas_call | solution.py:439
  71.3 1.0 %copy.10 = bf16[1,64,8192]{2,1,0:T(8,128)(2,1)} copy(bf16[1,64,8192]{2,1,0:T(8,128)(2,1)S(1)} %bitcast.7) | data formatting | bytes 2097152
  72.3 0.8 %copy.11 = bf16[1,1,8,2,8,2048]{5,4,3,2,1,0:T(8,128)(2,1)} copy(bf16[1,1,8,2,8,2048]{5,4,3,2,1,0:T(8,128)(2,1)S(1)} %bitcast.8) | data formatting | bytes 1048576
  (2 shorter events, 0.0 us)
Async XLA Ops:
  1.3 0.9 %copy-start.1 = (bf16[1,64,1024]{2,1,0:T(8,128)(2,1)S(1)}, bf16[1,64,1024]{2,1,0:T(8,128)(2,1)}, u32[]{:S(2)}) copy-start(bf16[1,64,1024]{2,1,0:T(8,128)(2,1)} %param.6) | copy-start | bytes 393220
  1.3 1.0 %copy-start.2 = (bf16[1,64,1024]{2,1,0:T(8,128)(2,1)S(1)}, bf16[1,64,1024]{2,1,0:T(8,128)(2,1)}, u32[]{:S(2)}) copy-start(bf16[1,64,1024]{2,1,0:T(8,128)(2,1)} %param.7) | copy-start | bytes 393220
  1.6 0.7 copy-start.3
  2.3 1.2 %copy-start = (bf16[1,64,8192]{2,1,0:T(8,128)(2,1)S(1)}, bf16[1,64,8192]{2,1,0:T(8,128)(2,1)}, u32[]{:S(2)}) copy-start(bf16[1,64,8192]{2,1,0:T(8,128)(2,1)} %param.5) | copy-start | bytes 3145732
